TPU v7x, 512 devices: a whole 4x8x8 slice. The times are simulated.
512 devices in a mesh: stream: 8 (over x, y_hi), expert: 64 (over z, y_lo, core).
Axes of the slice: x: 4, y: 8 (y_hi: 2, y_lo: 4; y = y_hi * 4 + y_lo), z: 8, core: 2. Of those that a mesh axis runs over, the one named last changes fastest.
Arguments:
- tokens: bfloat16 [32768, 2048], P(('stream', 'expert')), may hold values from -6 to 6
- route_gates: float32 [32768, 8], P(('stream', 'expert')), may hold values from 0.1 to 1
- expert_ids: int32 [32768, 8], P(('stream', 'expert')), may hold values from 0 to 63, as said below
- slot_index: int32 [32768, 8], P(('stream', 'expert')), may hold values from -1 to 7, as said below
- gate_quant: bfloat16 [64, 2048, 1024], P('expert', None, 'stream'), may hold values from -0.125 to 0.125
- up_quant: bfloat16 [64, 2048, 1024], P('expert', None, 'stream'), may hold values from -0.125 to 0.125
- down_quant: bfloat16 [64, 2048, 1024], P('expert', None, 'stream'), may hold values from -0.1875 to 0.1875
- gate_scale: float32 [64, 16, 8], P('expert', None, 'stream'), may hold values from 0.5 to 2
- up_scale: float32 [64, 16, 8], P('expert', None, 'stream'), may hold values from 0.5 to 2
- down_scale: float32 [64, 16, 8], P('expert', None, 'stream'), may hold values from 0.5 to 2
Outputs:
- mixed: bfloat16 [32768, 2048], P(('stream', 'expert'))
Inputs may be any that keep to these rules, and one draw needn't show every extreme that they name: `expert_ids`: the 8 ids of one token differ. `slot_index`: among the choices of one device's 64 tokens that name one expert, taken in token order, the first 8 get places 0, 1, ... and the rest get -1. In every draw some expert gets all 8 places from every device.
All inputs are finite; a program needn't handle non-finite values.
Results may differ from a plain program's by a relative error of at most 0.0076.
Values may be sent and summed in bfloat16 or wider, within the bound.
A program may use at most 64 MiB of HBM per device.

v0:
```python
import jax
import jax.numpy as jnp
from jax import lax
from jax.sharding import PartitionSpec as P

QB = 128


def dequantize(quant, scales):
    expanded = jnp.repeat(jnp.repeat(scales, QB, axis=0), QB, axis=1)
    return (quant.astype(jnp.float32) * expanded).astype(jnp.bfloat16)


def local(
    tokens,
    route_gates,
    expert_ids,
    slot_index,
    gate_quant,
    up_quant,
    down_quant,
    gate_scale,
    up_scale,
    down_scale,
):
    experts = lax.axis_size("expert")
    tok_rows = tokens.shape[0]
    top_count = expert_ids.shape[1]
    width = tokens.shape[1]
    capacity = max(2, tok_rows * top_count // experts)
    row_count = experts * capacity
    is_kept = slot_index >= 0
    position = jnp.where(is_kept, expert_ids * capacity + slot_index, -1)
    selector = jnp.any(
        position[None, :, :] == jnp.arange(row_count, dtype=jnp.int32)[:, None, None], axis=2
    )
    outgoing = jnp.dot(selector.astype(jnp.bfloat16), tokens, preferred_element_type=jnp.float32)
    outgoing = outgoing.astype(jnp.bfloat16).reshape(experts, capacity, width)
    incoming = lax.all_to_all(outgoing, "expert", split_axis=0, concat_axis=0, tiled=True).reshape(
        row_count, width
    )
    w_gate = dequantize(gate_quant[0], gate_scale[0])
    w_up = dequantize(up_quant[0], up_scale[0])
    w_down = dequantize(down_quant[0], down_scale[0])
    gate_piece = lax.all_gather(w_gate, "stream", axis=1, tiled=True)
    up_piece = lax.all_gather(w_up, "stream", axis=1, tiled=True)
    down_piece = lax.all_gather(w_down, "stream", axis=1, tiled=True)
    gate_act = jnp.dot(incoming, gate_piece, preferred_element_type=jnp.float32)
    up_act = jnp.dot(incoming, up_piece, preferred_element_type=jnp.float32)
    hidden = (jax.nn.silu(gate_act) * up_act).astype(jnp.bfloat16)
    running = jnp.einsum("rf,df->rd", hidden, down_piece, preferred_element_type=jnp.float32)
    expert_out = running.astype(jnp.bfloat16).reshape(experts, capacity, width)
    returned = lax.all_to_all(
        expert_out, "expert", split_axis=0, concat_axis=0, tiled=True
    ).reshape(row_count, width)
    gather_at = jnp.where(is_kept, position, 0).reshape(-1)
    picked = jnp.take(returned, gather_at, axis=0).reshape(tok_rows, top_count, width)
    weighting = jnp.where(is_kept, route_gates, jnp.float32(0.0))
    mixed_out = jnp.sum(weighting[:, :, None] * picked.astype(jnp.float32), axis=1)
    return mixed_out.astype(jnp.bfloat16)


def solution(mesh):
    return jax.shard_map(
        local,
        mesh=mesh,
        in_specs=(
            P(("stream", "expert"), None),
            P(("stream", "expert"), None),
            P(("stream", "expert"), None),
            P(("stream", "expert"), None),
            P("expert", None, "stream"),
            P("expert", None, "stream"),
            P("expert", None, "stream"),
            P("expert", None, "stream"),
            P("expert", None, "stream"),
            P("expert", None, "stream"),
        ),
        out_specs=P(("stream", "expert"), None),
        check_vma=False,
    )
```

profile of v0, /device:TPU:1, one launch (start us, length us, event | category | flops | bytes accessed | tf_op | source)
XLA Modules:
  0.0 463.8 jit_solution(14108242697115211861)
XLA Ops:
  6.5 0.0 copy-start
  6.5 0.0 all-gather.6.cloned.1.call-start
  6.5 0.8 broadcast_bitcast_fusion.1
  7.3 2.2 fusion.9
  9.5 0.0 all-gather.6.cloned.1.call-update
  9.6 0.0 all-gather.4.cloned.1.call-start
  9.6 0.7 broadcast_bitcast_fusion.2
  10.3 2.2 fusion.10
  12.5 0.0 all-gather.4.cloned.1.call-update
  12.5 0.0 all-gather.8.cloned.1.call-start
  12.6 0.0 copy-done.5
  12.6 0.1 broadcast_bitcast_fusion
  12.7 0.0 copy-done.1
  12.7 1.2 fusion.8
  13.8 0.0 all-gather.8.cloned.1.call-update
  13.9 0.0 copy-done.2
  13.9 0.1 copy.20
  14.0 0.4 fusion.11
  14.4 0.8 fusion
  15.1 120.6 %all_to_all.10 = bf16[64,8,2048]{2,1,0:T(8,128)(2,1)S(1)} all-to-all(bf16[64,8,2048]{2,1,0:T(8,128)(2,1)S(1)} %fusion), channel_id=1, replica_groups=mesh['stream'=8,'expert'=64] {'expert'}, dimensions={0} | all-to-all | bytes 4194304 | tf_op jit(solution)/shard_map/all_to_all | solution.py:39
  135.7 5.9 %fusion.2 = f32[512,1024]{1,0:T(8,128)} fusion(bf16[2048,1024]{1,0:T(8,128)(2,1)} %all-gather.6.cloned.1.call-done, bf16[64,8,2048]{2,1,0:T(8,128)(2,1)S(1)} %all_to_all.10), kind=kOutput, calls=%fused_computation.7 | convolution fusion | flops 2147483648 | bytes 8388608 | tf_op jit(solution)/shard_map/dot_general | solution.py:49
  141.6 119.7 %all-gather.4.cloned.1.call-done = bf16[2048,1024]{1,0:T(8,128)(2,1)} async-done(((bf16[2048,128]{1,0:T(8,128)(2,1)}), bf16[2048,1024]{1,0:T(8,128)(2,1)}) %all-gather.4.cloned.1.call-update) | async-done | bytes 4194320 | tf_op jit(solution)/shard_map/all_gather | solution.py:45
  261.3 116.1 %all-gather.8.cloned.1.call-done = bf16[2048,1024]{1,0:T(8,128)(2,1)} async-done(((bf16[2048,128]{1,0:T(8,128)(2,1)}), bf16[2048,1024]{1,0:T(8,128)(2,1)}) %all-gather.8.cloned.1.call-update) | async-done | bytes 4194320 | tf_op jit(solution)/shard_map/all_gather | solution.py:47
  377.4 10.2 %fusion.1 = bf16[64,8,2048]{2,1,0:T(8,128)(2,1)} fusion(bf16[2048,1024]{1,0:T(8,128)(2,1)} %all-gather.8.cloned.1.call-done, f32[512,1024]{1,0:T(8,128)} %fusion.2, bf16[2048,1024]{1,0:T(8,128)(2,1)} %all-gather.4.cloned.1.call-done, bf16[64,8,2048]{2,1,0:T(8,128)(2,1)S(1)} %all_to_all.10), kind=kOutput, calls=%fused_computation.5 | convolution fusion | flops 4299161600 | bytes 14680064 | tf_op jit(solution)/shard_map/rf,df->rd/dot_general | solution.py:51
  387.5 12.1 %all-to-all-start.1 = ((bf16[64,8,2048]{2,1,0:T(8,128)(2,1)}), bf16[64,8,2048]{2,1,0:T(8,128)(2,1)S(1)}, u32[]{:S(2)}, u32[]{:S(2)}) async-start(bf16[64,8,2048]{2,1,0:T(8,128)(2,1)} %fusion.1), calls=%async_computation.1 | async-start | bytes 4194304 | tf_op jit(solution)/shard_map/all_to_all | solution.py:53
  399.7 0.1 copy.21
  399.8 0.1 reshape.97
  399.9 0.1 copy.19
  400.0 0.1 copy.18
  400.1 49.2 %all-to-all-done.1 = bf16[64,8,2048]{2,1,0:T(8,128)(2,1)S(1)} async-done(((bf16[64,8,2048]{2,1,0:T(8,128)(2,1)}), bf16[64,8,2048]{2,1,0:T(8,128)(2,1)S(1)}, u32[]{:S(2)}, u32[]{:S(2)}) %all-to-all-start.1) | async-done | bytes 2097184 | tf_op jit(solution)/shard_map/all_to_all | solution.py:53
  449.3 3.3 gather_fusion
  452.7 4.7 %multiply_reduce_fusion = bf16[64,2048]{1,0:T(8,128)(2,1)} fusion(bf16[512,2048]{1,0:T(8,128)(2,1)} %gather_fusion, f32[64,8]{1,0:T(8,128)S(1)} %copy.18, pred[64,8]{1,0:T(8,128)(4,1)S(1)} %copy.19), kind=kLoop, calls=%fused_computation.1 | loop fusion | flops 4063232 | bytes 2361856 | tf_op jit(solution)/shard_map/reduce_sum | solution.py:59
  (14 shorter events, 0.1 us)
Async XLA Ops:
  6.5 7.8 %copy-start = (bf16[64,2048]{1,0:T(8,128)(2,1)S(1)}, bf16[64,2048]{1,0:T(8,128)(2,1)}, u32[]{:S(2)}) copy-start(bf16[64,2048]{1,0:T(8,128)(2,1)} %param.10) | copy-start | bytes 786436
  6.5 6.1 %copy-start.5 = (f32[1,16,1]{1,2,0:T(1,128)S(1)}, f32[1,16,1]{1,2,0:T(1,128)}, u32[]{:S(2)}) copy-start(f32[1,16,1]{1,2,0:T(1,128)} %param.19) | copy-start | bytes 196
  6.5 6.1 %copy-start.1 = (bf16[1,2048,128]{2,1,0:T(8,128)(2,1)S(1)}, bf16[1,2048,128]{2,1,0:T(8,128)(2,1)}, u32[]{:S(2)}) copy-start(bf16[1,2048,128]{2,1,0:T(8,128)(2,1)} %param.16) | copy-start | bytes 1572868
  6.5 129.2 %all-gather.6.cloned.1.call-start = ((), (), s32[]{:S(2)}) async-start(), calls=%async_computation.3 | async-start | bytes 4718592 | tf_op jit(solution)/shard_map/all_gather | solution.py:46
  9.5 4.3 copy-start.2
  9.5 4.3 copy-start.3
  9.6 251.7 %all-gather.4.cloned.1.call-start = ((), (), s32[]{:S(2)}) async-start(), calls=%async_computation.2 | async-start | bytes 4718592 | tf_op jit(solution)/shard_map/all_gather | solution.py:45
  12.5 364.8 %all-gather.8.cloned.1.call-start = ((), (), s32[]{:S(2)}) async-start(), calls=%async_computation.4 | async-start | bytes 4718592 | tf_op jit(solution)/shard_map/all_gather | solution.py:47
  387.5 12.4 %copy-start.4 = (f32[64,8]{0,1:T(8,128)S(1)}, f32[64,8]{0,1:T(8,128)}, u32[]{:S(2)}) copy-start(f32[64,8]{0,1:T(8,128)} %param.11) | copy-start | bytes 6148
  387.5 61.8 %all-to-all-start.1 = ((bf16[64,8,2048]{2,1,0:T(8,128)(2,1)}), bf16[64,8,2048]{2,1,0:T(8,128)(2,1)S(1)}, u32[]{:S(2)}, u32[]{:S(2)}) async-start(bf16[64,8,2048]{2,1,0:T(8,128)(2,1)} %fusion.1), calls=%async_computation.1 | async-start | bytes 4194304 | tf_op jit(solution)/shard_map/all_to_all | solution.py:53
Sparse Core Ops, SparseCore 0:
  10.4 114.8 all-gather.5
  128.4 132.8 all-gather.3
  264.4 112.9 all-gather.7
where the time goes:
time: 466 us; the launch traced here: 464 us
  waiting for transfers between devices  285 us (61%)
  blocking collectives  121 us (26%)
  matrix products  16.8 us (4%)
  between operations  13.2 us (3%)
  starting transfers between devices  12.2 us (3%)
  other arithmetic  10.6 us (2%)
  local copies, waits for them, and re-layouts  5.38 us (1%)
    all_to_all x1, blocking collectives, local(): lax.all_to_all(outgoing, 'expert', split_axis=0, concat_axis=0, tiled=True)  121 us
    all_gather x1, waiting for transfers between devices, local(): gate_piece = lax.all_gather(w_gate, 'stream', axis=1, tiled=True)  120 us
    all_gather x1, waiting for transfers between devices, local(): down_piece = lax.all_gather(w_down, 'stream', axis=1, tiled=True)  116 us
    all_to_all x1, waiting for transfers between devices, local(): lax.all_to_all(expert_out, 'expert', split_axis=0, concat_axis=0, tiled=T...  49.2 us
    all_to_all x1, starting transfers between devices, local(): lax.all_to_all(expert_out, 'expert', split_axis=0, concat_axis=0, tiled=T...  12.1 us
    dot_general x1, matrix products, local(): jnp.einsum('rf,df->rd', hidden, down_piece, preferred_element_type=jnp.fl...  10.2 us
  transfers between devices with their start and end apart: 4, of which 3 were waited for; matrix products, arithmetic and copies ran while one was open for 3% of the time, Pallas kernels for 0%

commit v1 on v0

v1 whole, which is shorter than its diff:
```python
import functools

import jax
import jax.numpy as jnp
from jax import lax
from jax.experimental import pallas as pl
from jax.experimental.pallas import tpu as pltpu
from jax.sharding import PartitionSpec as P

MESH = pl.DeviceIdType.MESH
F32 = jnp.float32
BF16 = jnp.bfloat16
GU_CHUNKS = 4
DN_CHUNKS = 2
CHUNKS = GU_CHUNKS + DN_CHUNKS
OFFSETS = (0, -1, 1, -2, 2, -3, 3, 4)
UP = (0, 1, 3, 5, 7)
DOWN = (0, 2, 4, 6, 7)


def kernel(
    tok, meta, sg, su, sd, gq, uq, dq, o_ref,
    tk, mt, ob, ib, gu, dn, lg, ld, hid, ans, ret, wh, wl, pt, rs_out, rs_in,
    w_send, w_recv, t_send, t_recv, m_send, m_recv, a_send, a_recv, b_send, b_recv, r_send, r_recv,
):
    stream, expert = lax.axis_index("stream"), lax.axis_index("expert")
    x, y_hi = stream // 2, stream % 2
    z, y_lo, core = expert // 8, (expert % 8) // 2, expert % 2
    y = 4 * y_hi + y_lo

    def dev(dx=0, dy=0, dz=0, dc=0):
        xx, yy, zz, cc = (x + dx + 4) % 4, (y + dy + 8) % 8, (z + dz + 8) % 8, (core + dc) % 2
        return (2 * xx + yy // 4, 8 * zz + 2 * (yy % 4) + cc)

    def rdma(src, dst, send, recv, device):
        return pltpu.make_async_remote_copy(
            src_ref=src, dst_ref=dst, send_sem=send, recv_sem=recv, device_id=device, device_id_type=MESH
        )

    swaps = core != y_hi
    barrier = pltpu.get_barrier_semaphore()
    peers = [dev(dx=1), dev(dx=-1), dev(dc=1), dev(dy=4, dc=1), dev(dy=1), dev(dy=-1)] + [dev(dz=k) for k in range(1, 8)]
    for peer in peers:
        pl.semaphore_signal(barrier, inc=1, device_id=peer, device_id_type=MESH)

    def dequantize(put_gu, put_dn):
        def block(b, carry):
            rows = pl.ds(pl.multiple_of(b * 128, 128), 128)
            put_gu(rows, 0, (gq[rows, :].astype(F32) * sg[b]).astype(BF16))
            put_gu(rows, 128, (uq[rows, :].astype(F32) * su[b]).astype(BF16))
            put_dn(rows, (dq[rows, :].astype(F32) * sd[b]).astype(BF16))
            return carry

        lax.fori_loop(0, 16, block, 0)

    @pl.when(swaps)
    def _():
        def put_gu(rows, lane, v):
            lg[rows, lane : lane + 128] = v

        def put_dn(rows, v):
            ld[rows, :] = v

        dequantize(put_gu, put_dn)

    @pl.when(jnp.logical_not(swaps))
    def _():
        def put_gu(rows, lane, v):
            gu[0, rows, lane : lane + 128] = v

        def put_dn(rows, v):
            dn[rows, 0:128] = v

        dequantize(put_gu, put_dn)

    tk[0] = tok[...]
    mt[0] = meta[...]
    pl.semaphore_wait(barrier, len(peers))

    def piece(slot, i, part=None):
        if i < GU_CHUNKS:
            rows = 2048 // GU_CHUNKS
            first = i * rows
        else:
            rows = 2048 // DN_CHUNKS
            first = (i - GU_CHUNKS) * rows
        if part is not None:
            rows //= 2
            first += part * rows
        if i < GU_CHUNKS:
            return gu.at[slot, pl.ds(first, rows), :]
        return dn.at[pl.ds(first, rows), pl.ds(slot * 128, 128)]

    def local_piece(i):
        if i < GU_CHUNKS:
            rows = 2048 // GU_CHUNKS
            return lg.at[pl.ds(i * rows, rows), :]
        rows = 2048 // DN_CHUNKS
        return ld.at[pl.ds((i - GU_CHUNKS) * rows, rows), :]

    def swap(i):
        return rdma(local_piece(i), piece(0, i), w_send.at[i, 0], w_recv.at[i, 0], dev(dy=4, dc=1))

    def own_up(i):
        return rdma(piece(0, i), piece(6, i), w_send.at[i, 1], w_recv.at[i, 1], dev(dx=1))

    def own_down(i):
        return rdma(piece(0, i), piece(2, i), w_send.at[i, 2], w_recv.at[i, 2], dev(dx=-1))

    def on_up(i):
        return rdma(piece(6, i, 0), piece(4, i, 0), w_send.at[i, 3], w_recv.at[i, 3], dev(dx=1))

    def on_down(i):
        return rdma(piece(2, i, 1), piece(4, i, 1), w_send.at[i, 4], w_recv.at[i, 4], dev(dx=-1))

    def share(i, r):
        return rdma(piece(2 * r, i), piece(2 * r + 1, i), w_send.at[i, 5 + r], w_recv.at[i, 5 + r], dev(dc=1))

    def tok_up(s):
        src, dst = tk.at[UP[s]], tk.at[UP[s + 1]]
        if s == 3:
            src, dst = src.at[pl.ds(0, 32), :], dst.at[pl.ds(0, 32), :]
        return rdma(src, dst, t_send.at[0, s], t_recv.at[0, s], dev(dy=1))

    def tok_down(s):
        src, dst = tk.at[DOWN[s]], tk.at[DOWN[s + 1]]
        if s == 3:
            src, dst = src.at[pl.ds(32, 32), :], dst.at[pl.ds(32, 32), :]
        return rdma(src, dst, t_send.at[1, s], t_recv.at[1, s], dev(dy=-1))

    def meta_up(s):
        return rdma(mt.at[UP[s]], mt.at[UP[s + 1]], m_send.at[0, s], m_recv.at[0, s], dev(dy=1))

    def meta_down(s):
        return rdma(mt.at[DOWN[s]], mt.at[DOWN[s + 1]], m_send.at[1, s], m_recv.at[1, s], dev(dy=-1))

    def token_start(s):
        tok_up(s).start()
        tok_down(s).start()
        meta_up(s).start()
        if s < 3:
            meta_down(s).start()

    def token_arrived(s):
        tok_up(s).wait_recv()
        tok_down(s).wait_recv()
        meta_up(s).wait_recv()
        if s < 3:
            meta_down(s).wait_recv()

    def there(p, k):
        rows = pl.ds(p * 128 + k * 16, 16)
        return rdma(ob.at[rows, :], ib.at[rows, :], a_send.at[p, k], a_recv.at[p, k], dev(dz=k))

    def back(p, k):
        rows = pl.ds(p * 128 + k * 16, 16)
        return rdma(ans.at[rows, :], ret.at[rows, :], b_send.at[p, k], b_recv.at[p, k], dev(dz=-k))

    def dispatch(p):
        row = lax.broadcasted_iota(jnp.int32, (128, 128), 0)
        lane = lax.broadcasted_iota(jnp.int32, (128, 128), 1)
        target = y * 64 + ((z + row // 16) % 8) * 8 + row % 8
        target = jnp.where((row % 16) // 8 == lane // 64, target, -5).astype(F32)
        half = lax.broadcasted_iota(jnp.int32, (16, 128), 1) // 64
        info = jnp.where(half == 0, mt[2 * p], mt[2 * p + 1])
        hit = jnp.zeros((128, 128), F32)
        weight = jnp.zeros((128, 128), F32)
        for k in range(8):
            same = target == info[k : k + 1, :]
            hit = jnp.where(same, 1.0, hit)
            weight = jnp.where(same, info[8 + k : 9 + k, :], weight)
        weight = weight.T
        high = weight.astype(BF16)
        wh[p] = high
        wl[p] = (weight - high.astype(F32)).astype(BF16)
        hit = hit.astype(BF16)
        for c in range(4):
            cols = pl.ds(c * 512, 512)
            both = jnp.concatenate([tk[2 * p, :, cols], tk[2 * p + 1, :, cols]], axis=0)
            ob[pl.ds(p * 128, 128), cols] = jnp.dot(hit, both, preferred_element_type=F32).astype(BF16)
        for k in range(1, 8):
            there(p, k).start()
        ib[pl.ds(p * 128, 16), :] = ob[pl.ds(p * 128, 16), :]

    token_start(0)

    @pl.when(swaps)
    def _():
        for i in range(CHUNKS):
            swap(i).start()

    @pl.when(jnp.logical_not(swaps))
    def _():
        for i in range(CHUNKS):
            own_up(i).start()
            own_down(i).start()
            share(i, 0).start()

    def own_round(i):
        @pl.when(swaps)
        def _():
            swap(i).wait_recv()
            own_up(i).start()
            own_down(i).start()
            share(i, 0).start()

    def forward_round(i):
        own_up(i).wait_recv()
        on_up(i).start()
        share(i, 3).start()
        own_down(i).wait_recv()
        on_down(i).start()
        share(i, 1).start()

    def far_round(i):
        on_up(i).wait_recv()
        on_down(i).wait_recv()
        share(i, 2).start()

    token_arrived(0)
    token_start(1)
    dispatch(0)
    own_round(0)
    forward_round(0)
    token_arrived(1)
    token_start(2)
    dispatch(1)
    own_round(1)
    forward_round(1)
    far_round(0)
    token_arrived(2)
    token_start(3)
    dispatch(2)
    own_round(2)
    forward_round(2)
    far_round(1)
    own_round(3)
    forward_round(3)
    far_round(2)
    token_arrived(3)
    dispatch(3)
    own_round(4)
    forward_round(4)
    far_round(3)
    own_round(5)
    forward_round(5)
    far_round(4)
    for i in range(GU_CHUNKS):
        for r in range(4):
            share(i, r).wait_recv()
    for p in range(4):
        for k in range(1, 8):
            there(p, k).wait_recv()
    far_round(5)

    def hidden_step(s, carry):
        for m in range(2):
            rows = pl.ds(m * 256, 256)
            both = jnp.dot(ib[rows, :], gu[s], preferred_element_type=F32)
            g, u = both[:, :128], both[:, 128:]
            h = g / (1.0 + jnp.exp(-g)) * u
            hid[rows, pl.ds(pl.multiple_of(s * 128, 128), 128)] = h.astype(BF16)
        return carry

    lax.fori_loop(0, 8, hidden_step, 0)
    for i in range(GU_CHUNKS, CHUNKS):
        for r in range(4):
            share(i, r).wait_recv()

    for p in (3, 2, 1, 0):
        rows = pl.ds(p * 128, 128)

        def answer_step(c, carry, rows=rows):
            cols = pl.ds(pl.multiple_of(c * 256, 256), 256)
            a = lax.dot_general(hid[rows, :], dn[cols, :], (((1,), (1,)), ((), ())), preferred_element_type=F32)
            ans[rows, cols] = a.astype(BF16)
            return carry

        lax.fori_loop(0, 8, answer_step, 0)
        for k in (4, 3, 5, 2, 6, 1, 7):
            back(p, k).start()
        ret[pl.ds(p * 128, 16), :] = ans[pl.ds(p * 128, 16), :]

    def sum_up(s):
        rows = pl.ds(0, 32 if s == 0 else 64)
        return rdma(rs_out.at[0, s, rows, :], rs_in.at[0, s, rows, :], r_send.at[0, s], r_recv.at[0, s], dev(dy=1))

    def sum_down(s):
        rows = pl.ds(32, 32) if s == 0 else pl.ds(0, 64)
        return rdma(rs_out.at[1, s, rows, :], rs_in.at[1, s, rows, :], r_send.at[1, s], r_recv.at[1, s], dev(dy=-1))

    def combine(p):
        for k in range(1, 8):
            back(p, k).wait_recv()
        for c in range(4):
            cols = pl.ds(c * 512, 512)
            r = ret[pl.ds(p * 128, 128), cols]
            pt[:, cols] = jnp.dot(wh[p], r, preferred_element_type=F32) + jnp.dot(wl[p], r, preferred_element_type=F32)

    def add_up(s, first):
        sum_up(s - 1).wait_recv()
        if s == 1:
            rs_out[0, s, 0:32, :] = (pt[first : first + 32, :] + rs_in[0, 0, 0:32, :].astype(F32)).astype(BF16)
            rs_out[0, s, 32:64, :] = pt[first + 32 : first + 64, :].astype(BF16)
        else:
            rs_out[0, s] = (pt[first : first + 64, :] + rs_in[0, s - 1].astype(F32)).astype(BF16)
        sum_up(s).start()

    def add_down(s, first):
        sum_down(s - 1).wait_recv()
        if s == 1:
            rs_out[1, s, 0:32, :] = pt[first : first + 32, :].astype(BF16)
            rs_out[1, s, 32:64, :] = (pt[first + 32 : first + 64, :] + rs_in[1, 0, 32:64, :].astype(F32)).astype(BF16)
        else:
            rs_out[1, s] = (pt[first : first + 64, :] + rs_in[1, s - 1].astype(F32)).astype(BF16)
        sum_down(s).start()

    combine(3)
    rs_out[0, 0, 0:32, :] = pt[64:96, :].astype(BF16)
    rs_out[1, 0, 32:64, :] = pt[96:128, :].astype(BF16)
    sum_up(0).start()
    sum_down(0).start()
    add_up(1, 0)
    combine(2)
    add_up(2, 0)
    add_down(1, 64)
    combine(1)
    add_up(3, 0)
    add_down(2, 64)
    combine(0)
    add_down(3, 64)
    sum_up(3).wait_recv()
    sum_down(3).wait_recv()
    o_ref[...] = (pt[0:64, :] + rs_in[0, 3].astype(F32) + rs_in[1, 3].astype(F32)).astype(BF16)

    @pl.when(swaps)
    def _():
        for i in range(CHUNKS):
            swap(i).wait_send()

    for i in range(CHUNKS):
        own_up(i).wait_send()
        own_down(i).wait_send()
        on_up(i).wait_send()
        on_down(i).wait_send()
        for r in range(4):
            share(i, r).wait_send()
    for s in range(4):
        tok_up(s).wait_send()
        tok_down(s).wait_send()
        meta_up(s).wait_send()
        if s < 3:
            meta_down(s).wait_send()
        sum_up(s).wait_send()
        sum_down(s).wait_send()
    for p in range(4):
        for k in range(1, 8):
            there(p, k).wait_send()
            back(p, k).wait_send()


def local(
    tokens,
    route_gates,
    expert_ids,
    slot_index,
    gate_quant,
    up_quant,
    down_quant,
    gate_scale,
    up_scale,
    down_scale,
):
    y_of = (expert_ids % 2) * 4 + (expert_ids // 2) % 4
    code = jnp.where(slot_index >= 0, y_of * 64 + (expert_ids // 8) * 8 + slot_index, -1).astype(F32)
    info = jnp.concatenate([code, route_gates], axis=1).T
    info = jnp.concatenate([info, info], axis=1)
    vmem = pl.BlockSpec(memory_space=pltpu.VMEM)
    smem = pl.BlockSpec(memory_space=pltpu.SMEM)
    dma = pltpu.SemaphoreType.DMA
    return pl.pallas_call(
        kernel,
        out_shape=jax.ShapeDtypeStruct((64, 2048), BF16),
        in_specs=[vmem, vmem, smem, smem, smem, vmem, vmem, vmem],
        out_specs=vmem,
        scratch_shapes=[
            pltpu.VMEM((8, 64, 2048), BF16),
            pltpu.VMEM((8, 16, 128), F32),
            pltpu.VMEM((512, 2048), BF16),
            pltpu.VMEM((512, 2048), BF16),
            pltpu.VMEM((8, 2048, 256), BF16),
            pltpu.VMEM((2048, 1024), BF16),
            pltpu.VMEM((2048, 256), BF16),
            pltpu.VMEM((2048, 128), BF16),
            pltpu.VMEM((512, 1024), BF16),
            pltpu.VMEM((512, 2048), BF16),
            pltpu.VMEM((512, 2048), BF16),
            pltpu.VMEM((4, 128, 128), BF16),
            pltpu.VMEM((4, 128, 128), BF16),
            pltpu.VMEM((128, 2048), F32),
            pltpu.VMEM((2, 4, 64, 2048), BF16),
            pltpu.VMEM((2, 4, 64, 2048), BF16),
            dma((CHUNKS, 9)),
            dma((CHUNKS, 9)),
            dma((2, 4)),
            dma((2, 4)),
            dma((2, 4)),
            dma((2, 4)),
            dma((4, 8)),
            dma((4, 8)),
            dma((4, 8)),
            dma((4, 8)),
            dma((2, 4)),
            dma((2, 4)),
        ],
        compiler_params=pltpu.CompilerParams(
            collective_id=0, has_side_effects=True, vmem_limit_bytes=56 * 2**20
        ),
        name="experts",
    )(
        tokens,
        info,
        gate_scale.reshape(16),
        up_scale.reshape(16),
        down_scale.reshape(16),
        gate_quant[0],
        up_quant[0],
        down_quant[0],
    )


def solution(mesh):
    return jax.shard_map(
        local,
        mesh=mesh,
        in_specs=(
            P(("stream", "expert"), None),
            P(("stream", "expert"), None),
            P(("stream", "expert"), None),
            P(("stream", "expert"), None),
            P("expert", None, "stream"),
            P("expert", None, "stream"),
            P("expert", None, "stream"),
            P("expert", None, "stream"),
            P("expert", None, "stream"),
            P("expert", None, "stream"),
        ),
        out_specs=P(("stream", "expert"), None),
        check_vma=False,
    )
```

time: 466 us -> 173 us (0.37)
  waiting for transfers between devices: 285 us -> 0 us
  Pallas kernels: 0 us -> 169 us
  blocking collectives: 121 us -> 0 us
  matrix products: 16.8 us -> 0 us
  between operations: 13.2 us -> 0.01 us
  starting transfers between devices: 12.2 us -> 0 us
  other arithmetic: 10.6 us -> 0.7 us
    all_gather x3 -> x0, waiting for transfers between devices: 236 us -> none  [the longest x1 120 us: local(): gate_piece = lax.all_gather(w_gate, 'stream', axis=1, tiled=True)]
    pallas_call x0 -> x1, Pallas kernels: none -> 169 us  [local(): pl.pallas_call(kernel, out_shape=jax.ShapeDtypeStruct((64, 2048), BF16),...]
    all_to_all x1 -> x0, blocking collectives: 121 us -> none  [local(): lax.all_to_all(outgoing, 'expert', split_axis=0, concat_axis=0, tiled=True)]
    all_to_all x1 -> x0, waiting for transfers between devices: 49.2 us -> none  [local(): lax.all_to_all(expert_out, 'expert', split_axis=0, concat_axis=0, tiled=T...]
    dot_general x3 -> x0, matrix products: 16.8 us -> none  [the longest x1 10.2 us: local(): jnp.einsum('rf,df->rd', hidden, down_piece, preferred_element_type=jnp.fl...]
    all_to_all x1 -> x0, starting transfers between devices: 12.1 us -> none  [local(): lax.all_to_all(expert_out, 'expert', split_axis=0, concat_axis=0, tiled=T...]
    convert_element_type x3 -> x1, other arithmetic: 5.53 us -> 0.02 us  [local(): jnp.where(slot_index >= 0, y_of * 64 + expert_ids // 8 * 8 + slot_index, -1)]
    reduce_sum x1 -> x0, other arithmetic: 4.67 us -> none  [local(): jnp.sum(weighting[:, :, None] * picked.astype(jnp.float32), axis=1)]
  transfers between devices with their start and end apart: 4 -> 0, of which waited for: 3 -> 0; matrix products, arithmetic and copies ran while one was open for 3% -> 0% of each run, Pallas kernels for 0% -> 0%
where the time goes in v1:
time: 173 us
  Pallas kernels  169 us (98%)
  local copies, waits for them, and re-layouts  3.03 us (2%)
    pallas_call x1, Pallas kernels, local(): pl.pallas_call(kernel, out_shape=jax.ShapeDtypeStruct((64, 2048), BF16),...  169 us

profile of v1, /device:TPU:1, one launch (start us, length us, event | category | flops | bytes accessed | tf_op | source)
XLA Modules:
  0.0 173.2 jit_solution(388792062958118540)
XLA Ops:
  0.0 0.0 copy-start.1
  0.0 0.0 copy-start
  0.0 0.7 copy-done.1
  0.7 0.0 copy-done
  0.7 0.0 copy-start.2
  0.7 0.7 copy-done.2
  1.4 0.7 pad_maximum_fusion.meta
  2.1 169.4 %experts.1 = bf16[64,2048]{1,0:T(8,128)(2,1)} custom-call(bf16[64,2048]{1,0:T(8,128)(2,1)} %tok.1, f32[16,128]{1,0:T(8,128)} %pad_maximum_fusion.meta, f32[16]{0:T(128)} %bitcast.11, f32[16]{0:T(128)} %bitcast.12, f32[16]{0:T(128)} %bitcast.13, bf16[2048,128]{1,0:T(8,128)(2,1)} %bitcast.8, bf16[2048,128]{1,0:T(8,128)(2,1)} %bitcast.9, bf16[2048,128]{1,0:T(8,128)(2,1)} %bitcast.10), custom_call_target="tpu_custom_call" | custom-call | tf_op jit(solution)/shard_map/experts/pallas_call | solution.py:381
  171.5 1.7 copy.12
  (2 shorter events, 0.0 us)
Async XLA Ops:
  0.0 0.7 copy-start.1
  0.0 0.7 copy-start
  0.7 0.7 copy-start.2

commit v2 on v1

v2 whole, which is shorter than its diff:
```python
import functools

import jax
import jax.numpy as jnp
from jax import lax
from jax.experimental import pallas as pl
from jax.experimental.pallas import tpu as pltpu
from jax.sharding import PartitionSpec as P

MESH = pl.DeviceIdType.MESH
F32 = jnp.float32
BF16 = jnp.bfloat16
GU_CHUNKS = 4
DN_CHUNKS = 2
CHUNKS = GU_CHUNKS + DN_CHUNKS
TOKEN_TIMES = (8.0, 17.0, 25.0, 32.0)
A_FIRST, A_STEP, A_FAR = 6.0, 4.0, 5.0
SWAP_WINDOW = 2
OWN_WINDOW = 2
B_FIRST, B_STEP, B_NEXT, B_FAR = 9.0, 7.0, 7.5, 7.0
Z_ORDER = (7, 6, 5, 4, 3, 2, 1)
OFFSETS = (0, -1, 1, -2, 2, -3, 3, 4)
UP = (0, 1, 3, 5, 7)
DOWN = (0, 2, 4, 6, 7)


def kernel(
    tok, meta, sg, su, sd, gq, uq, dq, o_ref,
    tk, mt, mz, ob, ib, gu, dn, lg, ld, hid, lhs, ans, ret, wh, wl, pt, rs_out, rs_in,
    w_send, w_recv, t_send, t_recv, m_send, m_recv, n_send, n_recv, a_send, a_recv, b_send, b_recv, r_send, r_recv,
):
    stream, expert = lax.axis_index("stream"), lax.axis_index("expert")
    x, y_hi = stream // 2, stream % 2
    z, y_lo, core = expert // 8, (expert % 8) // 2, expert % 2
    y = 4 * y_hi + y_lo

    def dev(dx=0, dy=0, dz=0, dc=0):
        xx, yy, zz, cc = (x + dx + 4) % 4, (y + dy + 8) % 8, (z + dz + 8) % 8, (core + dc) % 2
        return (2 * xx + yy // 4, 8 * zz + 2 * (yy % 4) + cc)

    def rdma(src, dst, send, recv, device):
        return pltpu.make_async_remote_copy(
            src_ref=src, dst_ref=dst, send_sem=send, recv_sem=recv, device_id=device, device_id_type=MESH
        )

    swaps = core != y_hi
    barrier = pltpu.get_barrier_semaphore()
    peers = [dev(dx=1), dev(dx=-1), dev(dc=1), dev(dy=4, dc=1)]
    peers += [dev(dy=k) for k in range(1, 8)] + [dev(dz=k) for k in range(1, 8)]
    for peer in peers:
        pl.semaphore_signal(barrier, inc=1, device_id=peer, device_id_type=MESH)

    def dequantize(i):
        if i < GU_CHUNKS:
            n, first = 16 // GU_CHUNKS, i * (16 // GU_CHUNKS)
        else:
            n, first = 16 // DN_CHUNKS, (i - GU_CHUNKS) * (16 // DN_CHUNKS)

        def fill(gu_ref, dn_ref):
            def block(b, carry):
                rows = pl.ds(pl.multiple_of(b * 128, 128), 128)
                if i < GU_CHUNKS:
                    gu_ref[rows, 0:128] = (gq[rows, :].astype(F32) * sg[b]).astype(BF16)
                    gu_ref[rows, 128:256] = (uq[rows, :].astype(F32) * su[b]).astype(BF16)
                else:
                    dn_ref[rows, :] = (dq[rows, :].astype(F32) * sd[b]).astype(BF16)
                return carry

            lax.fori_loop(first, first + n, block, 0)

        pl.when(swaps)(lambda: fill(lg, ld))
        pl.when(jnp.logical_not(swaps))(lambda: fill(gu.at[0], dn.at[0]))

    tk[0] = tok[...]
    mt[0] = meta[...]
    mz[0] = meta[...]
    for i in range(CHUNKS):
        dequantize(i)
    pl.semaphore_wait(barrier, len(peers))

    def piece(slot, i, part=None):
        if i < GU_CHUNKS:
            rows = 2048 // GU_CHUNKS
            first = i * rows
        else:
            rows = 2048 // DN_CHUNKS
            first = (i - GU_CHUNKS) * rows
        if part is not None:
            rows //= 2
            first += part * rows
        if i < GU_CHUNKS:
            return gu.at[slot, pl.ds(first, rows), :]
        return dn.at[slot, pl.ds(first, rows), :]

    def local_piece(i):
        if i < GU_CHUNKS:
            rows = 2048 // GU_CHUNKS
            return lg.at[pl.ds(i * rows, rows), :]
        rows = 2048 // DN_CHUNKS
        return ld.at[pl.ds((i - GU_CHUNKS) * rows, rows), :]

    def swap(i):
        return rdma(local_piece(i), piece(0, i), w_send.at[i, 0], w_recv.at[i, 0], dev(dy=4, dc=1))

    def own_up(i):
        return rdma(piece(0, i), piece(6, i), w_send.at[i, 1], w_recv.at[i, 1], dev(dx=1))

    def own_down(i):
        return rdma(piece(0, i), piece(2, i), w_send.at[i, 2], w_recv.at[i, 2], dev(dx=-1))

    def on_up(i):
        return rdma(piece(6, i, 0), piece(4, i, 0), w_send.at[i, 3], w_recv.at[i, 3], dev(dx=1))

    def on_down(i):
        return rdma(piece(2, i, 1), piece(4, i, 1), w_send.at[i, 4], w_recv.at[i, 4], dev(dx=-1))

    def share(i, r):
        return rdma(piece(2 * r, i), piece(2 * r + 1, i), w_send.at[i, 5 + r], w_recv.at[i, 5 + r], dev(dc=1))

    def tok_up(s):
        src, dst = tk.at[UP[s]], tk.at[UP[s + 1]]
        if s == 3:
            src, dst = src.at[pl.ds(0, 32), :], dst.at[pl.ds(0, 32), :]
        return rdma(src, dst, t_send.at[0, s], t_recv.at[0, s], dev(dy=1))

    def tok_down(s):
        src, dst = tk.at[DOWN[s]], tk.at[DOWN[s + 1]]
        if s == 3:
            src, dst = src.at[pl.ds(32, 32), :], dst.at[pl.ds(32, 32), :]
        return rdma(src, dst, t_send.at[1, s], t_recv.at[1, s], dev(dy=-1))

    def meta_up(s):
        return rdma(mt.at[UP[s]], mt.at[UP[s + 1]], m_send.at[0, s], m_recv.at[0, s], dev(dy=1))

    def meta_down(s):
        return rdma(mt.at[DOWN[s]], mt.at[DOWN[s + 1]], m_send.at[1, s], m_recv.at[1, s], dev(dy=-1))

    def token_start(s):
        tok_up(s).start()
        tok_down(s).start()
        meta_up(s).start()
        if s < 3:
            meta_down(s).start()

    def token_arrived(s):
        tok_up(s).wait_recv()
        tok_down(s).wait_recv()
        meta_up(s).wait_recv()
        if s < 3:
            meta_down(s).wait_recv()

    def meta_z(k):
        return rdma(mt.at[0], mz.at[k], n_send.at[k], n_recv.at[k], dev(dz=-OFFSETS[k]))

    def there(p, k):
        rows = pl.ds(p * 128 + k * 16, 16)
        return rdma(ob.at[rows, :], ib.at[rows, :], a_send.at[p, k], a_recv.at[p, k], dev(dz=-OFFSETS[k]))

    def back(h, p, k):
        rows = pl.ds(p * 128 + k * 16, 16)
        to = dev(dz=OFFSETS[k]) if h == 0 else dev(dy=OFFSETS[k])
        return rdma(ans.at[h, rows, :], ret.at[h, rows, :], b_send.at[h, p, k], b_recv.at[h, p, k], to)

    def weigh(h, p):
        gathered = mt if h == 0 else mz
        row = lax.broadcasted_iota(jnp.int32, (128, 128), 0)
        lane = lax.broadcasted_iota(jnp.int32, (128, 128), 1)
        block = row // 16
        off = jnp.where(block % 2 == 1, -((block + 1) // 2), block // 2)
        if h == 0:
            target = y * 64 + ((z - off + 8) % 8) * 8 + row % 8
        else:
            target = ((y - off + 8) % 8) * 64 + z * 8 + row % 8
        target = jnp.where((row % 16) // 8 == lane // 64, target, -5).astype(F32)
        half = lax.broadcasted_iota(jnp.int32, (16, 128), 1) // 64
        info = jnp.where(half == 0, gathered[2 * p], gathered[2 * p + 1])
        hit = jnp.zeros((128, 128), F32)
        weight = jnp.zeros((128, 128), F32)
        for k in range(8):
            same = target == info[k : k + 1, :]
            hit = jnp.where(same, 1.0, hit)
            weight = jnp.where(same, info[8 + k : 9 + k, :], weight)
        weight = weight.T
        high = weight.astype(BF16)
        wh[h, p] = high
        wl[h, p] = (weight - high.astype(F32)).astype(BF16)
        return hit.astype(BF16)

    def dispatch(p):
        hit = weigh(0, p)
        for c in range(4):
            cols = pl.ds(c * 512, 512)
            both = jnp.concatenate([tk[2 * p, :, cols], tk[2 * p + 1, :, cols]], axis=0)
            ob[pl.ds(p * 128, 128), cols] = jnp.dot(hit, both, preferred_element_type=F32).astype(BF16)
        for k in Z_ORDER:
            there(p, k).start()
        ib[pl.ds(p * 128, 16), :] = ob[pl.ds(p * 128, 16), :]

    def own_start(i):
        own_up(i).start()
        own_down(i).start()
        share(i, 0).start()

    token_start(0)
    for k in range(1, 8):
        meta_z(k).start()

    @pl.when(swaps)
    def _():
        for i in range(SWAP_WINDOW):
            swap(i).start()

    @pl.when(jnp.logical_not(swaps))
    def _():
        for i in range(OWN_WINDOW):
            own_start(i)

    def own_round(i):
        swap(i).wait_recv()
        if i + SWAP_WINDOW < CHUNKS:
            swap(i + SWAP_WINDOW).start()
        own_start(i)

    def forward_round(i, more=False):
        own_up(i).wait_recv()
        on_up(i).start()
        own_down(i).wait_recv()
        on_down(i).start()
        if more and i + OWN_WINDOW < CHUNKS:
            own_start(i + OWN_WINDOW)
        share(i, 3).start()
        share(i, 1).start()

    def far_round(i):
        on_up(i).wait_recv()
        on_down(i).wait_recv()
        share(i, 2).start()

    def token_round(s):
        token_arrived(s)
        if s < 3:
            token_start(s + 1)
        dispatch(s)

    def run(events):
        def some():
            for event, i in events:
                event(i)

        return some

    kept, swapped = [], []
    for i in range(CHUNKS):
        t = A_FIRST + A_STEP * i
        kept += [(t, functools.partial(forward_round, more=True), i), (t + A_FAR, far_round, i)]
        t = B_FIRST + B_STEP * i
        swapped += [(t, own_round, i), (t + B_NEXT, forward_round, i), (t + B_NEXT + B_FAR, far_round, i)]
    order = lambda event: event[0]
    kept, swapped = sorted(kept, key=order), sorted(swapped, key=order)
    since = -1.0
    for s, until in enumerate(TOKEN_TIMES + (1e9,)):
        pl.when(jnp.logical_not(swaps))(run([e[1:] for e in kept if since <= e[0] < until]))
        pl.when(swaps)(run([e[1:] for e in swapped if since <= e[0] < until]))
        since = until
        if s < 4:
            token_round(s)
    for i in range(GU_CHUNKS):
        for r in range(4):
            share(i, r).wait_recv()
    for p in range(4):
        for k in range(1, 8):
            there(p, k).wait_recv()

    for k in range(1, 8):
        meta_z(k).wait_recv()
    for p in range(4):
        weigh(1, p)

    def hidden_step(s, carry):
        for m in range(2):
            rows = pl.ds(m * 256, 256)
            both = jnp.dot(ib[rows, :], gu[s], preferred_element_type=F32)
            g, u = both[:, :128], both[:, 128:]
            hid[rows, pl.ds(pl.multiple_of(s * 128, 128), 128)] = g / (1.0 + jnp.exp(-g)) * u
        return carry

    lax.fori_loop(0, 8, hidden_step, 0)
    for i in range(GU_CHUNKS, CHUNKS):
        for r in range(4):
            share(i, r).wait_recv()

    for p in (3, 2, 1, 0):
        for h in range(2):
            if h == 0:
                lhs[...] = hid[pl.ds(p * 128, 128), :].astype(BF16)
            else:
                for q in range(4):
                    first = q * 128 + p * 32
                    part = [hid[pl.ds(first + g, 8), :] for g in (0, 16, 8, 24)]
                    lhs[pl.ds(q * 32, 32), :] = jnp.concatenate(part, axis=0).astype(BF16)

            def answer_step(c, carry, h=h, p=p):
                first = pl.multiple_of(c * 256, 256)
                down = jnp.concatenate([dn[s, pl.ds(h * 1024 + first, 256), :] for s in range(8)], axis=1)
                a = lax.dot_general(lhs[...], down, (((1,), (1,)), ((), ())), preferred_element_type=F32)
                ans[h, pl.ds(p * 128, 128), pl.ds(first, 256)] = a.astype(BF16)
                return carry

            lax.fori_loop(0, 4, answer_step, 0)
            for k in Z_ORDER:
                back(h, p, k).start()
            ret[h, pl.ds(p * 128, 16), :] = ans[h, pl.ds(p * 128, 16), :]

    def sum_up(h, s):
        rows = pl.ds(0, 32 if s == 0 else 64)
        to = dev(dy=1) if h == 0 else dev(dz=1)
        return rdma(rs_out.at[h, 0, s, rows, :], rs_in.at[h, 0, s, rows, :], r_send.at[h, 0, s], r_recv.at[h, 0, s], to)

    def sum_down(h, s):
        rows = pl.ds(32, 32) if s == 0 else pl.ds(0, 64)
        to = dev(dy=-1) if h == 0 else dev(dz=-1)
        return rdma(rs_out.at[h, 1, s, rows, :], rs_in.at[h, 1, s, rows, :], r_send.at[h, 1, s], r_recv.at[h, 1, s], to)

    def combine(h, p):
        for k in range(1, 8):
            back(h, p, k).wait_recv()
        for c in range(2):
            cols = pl.ds(c * 512, 512)
            r = ret[h, pl.ds(p * 128, 128), cols]
            high = jnp.dot(wh[h, p], r, preferred_element_type=F32)
            pt[h, :, cols] = high + jnp.dot(wl[h, p], r, preferred_element_type=F32)

    def add_up(h, s, first):
        sum_up(h, s - 1).wait_recv()
        if s == 1:
            rs_out[h, 0, s, 0:32, :] = (pt[h, first : first + 32, :] + rs_in[h, 0, 0, 0:32, :].astype(F32)).astype(BF16)
            rs_out[h, 0, s, 32:64, :] = pt[h, first + 32 : first + 64, :].astype(BF16)
        else:
            rs_out[h, 0, s] = (pt[h, first : first + 64, :] + rs_in[h, 0, s - 1].astype(F32)).astype(BF16)
        sum_up(h, s).start()

    def add_down(h, s, first):
        sum_down(h, s - 1).wait_recv()
        if s == 1:
            rs_out[h, 1, s, 0:32, :] = pt[h, first : first + 32, :].astype(BF16)
            last = pt[h, first + 32 : first + 64, :] + rs_in[h, 1, 0, 32:64, :].astype(F32)
            rs_out[h, 1, s, 32:64, :] = last.astype(BF16)
        else:
            rs_out[h, 1, s] = (pt[h, first : first + 64, :] + rs_in[h, 1, s - 1].astype(F32)).astype(BF16)
        sum_down(h, s).start()

    for h in range(2):
        combine(h, 3)
        rs_out[h, 0, 0, 0:32, :] = pt[h, 64:96, :].astype(BF16)
        rs_out[h, 1, 0, 32:64, :] = pt[h, 96:128, :].astype(BF16)
        sum_up(h, 0).start()
        sum_down(h, 0).start()
    for h in range(2):
        add_up(h, 1, 0)
    for h in range(2):
        combine(h, 2)
        add_down(h, 1, 64)
        add_up(h, 2, 0)
    for h in range(2):
        combine(h, 1)
        add_down(h, 2, 64)
        add_up(h, 3, 0)
    for h in range(2):
        combine(h, 0)
        add_down(h, 3, 64)
    for h in range(2):
        sum_up(h, 3).wait_recv()
        sum_down(h, 3).wait_recv()
        total = pt[h, 0:64, :] + rs_in[h, 0, 3].astype(F32) + rs_in[h, 1, 3].astype(F32)
        o_ref[:, h * 1024 : h * 1024 + 1024] = total.astype(BF16)

    @pl.when(swaps)
    def _():
        for i in range(CHUNKS):
            swap(i).wait_send()

    for i in range(CHUNKS):
        own_up(i).wait_send()
        own_down(i).wait_send()
        on_up(i).wait_send()
        on_down(i).wait_send()
        for r in range(4):
            share(i, r).wait_send()
    for s in range(4):
        tok_up(s).wait_send()
        tok_down(s).wait_send()
        meta_up(s).wait_send()
        if s < 3:
            meta_down(s).wait_send()
        for h in range(2):
            sum_up(h, s).wait_send()
            sum_down(h, s).wait_send()
    for k in range(1, 8):
        meta_z(k).wait_send()
        for p in range(4):
            there(p, k).wait_send()
            for h in range(2):
                back(h, p, k).wait_send()


def local(
    tokens,
    route_gates,
    expert_ids,
    slot_index,
    gate_quant,
    up_quant,
    down_quant,
    gate_scale,
    up_scale,
    down_scale,
):
    y_of = (expert_ids % 2) * 4 + (expert_ids // 2) % 4
    code = jnp.where(slot_index >= 0, y_of * 64 + (expert_ids // 8) * 8 + slot_index, -1).astype(F32)
    info = jnp.concatenate([code, route_gates], axis=1).T
    info = jnp.concatenate([info, info], axis=1)
    vmem = pl.BlockSpec(memory_space=pltpu.VMEM)
    smem = pl.BlockSpec(memory_space=pltpu.SMEM)
    dma = pltpu.SemaphoreType.DMA
    return pl.pallas_call(
        kernel,
        out_shape=jax.ShapeDtypeStruct((64, 2048), BF16),
        in_specs=[vmem, vmem, smem, smem, smem, vmem, vmem, vmem],
        out_specs=vmem,
        scratch_shapes=[
            pltpu.VMEM((8, 64, 2048), BF16),
            pltpu.VMEM((8, 16, 128), F32),
            pltpu.VMEM((8, 16, 128), F32),
            pltpu.VMEM((512, 2048), BF16),
            pltpu.VMEM((512, 2048), BF16),
            pltpu.VMEM((8, 2048, 256), BF16),
            pltpu.VMEM((8, 2048, 128), BF16),
            pltpu.VMEM((2048, 256), BF16),
            pltpu.VMEM((2048, 128), BF16),
            pltpu.VMEM((512, 1024), F32),
            pltpu.VMEM((128, 1024), BF16),
            pltpu.VMEM((2, 512, 1024), BF16),
            pltpu.VMEM((2, 512, 1024), BF16),
            pltpu.VMEM((2, 4, 128, 128), BF16),
            pltpu.VMEM((2, 4, 128, 128), BF16),
            pltpu.VMEM((2, 128, 1024), F32),
            pltpu.VMEM((2, 2, 4, 64, 1024), BF16),
            pltpu.VMEM((2, 2, 4, 64, 1024), BF16),
            dma((CHUNKS, 9)),
            dma((CHUNKS, 9)),
            dma((2, 4)),
            dma((2, 4)),
            dma((2, 4)),
            dma((2, 4)),
            dma((8,)),
            dma((8,)),
            dma((4, 8)),
            dma((4, 8)),
            dma((2, 4, 8)),
            dma((2, 4, 8)),
            dma((2, 2, 4)),
            dma((2, 2, 4)),
        ],
        compiler_params=pltpu.CompilerParams(
            collective_id=0, has_side_effects=True, vmem_limit_bytes=56 * 2**20
        ),
        name="experts",
    )(
        tokens,
        info,
        gate_scale.reshape(16),
        up_scale.reshape(16),
        down_scale.reshape(16),
        gate_quant[0],
        up_quant[0],
        down_quant[0],
    )


def solution(mesh):
    return jax.shard_map(
        local,
        mesh=mesh,
        in_specs=(
            P(("stream", "expert"), None),
            P(("stream", "expert"), None),
            P(("stream", "expert"), None),
            P(("stream", "expert"), None),
            P("expert", None, "stream"),
            P("expert", None, "stream"),
            P("expert", None, "stream"),
            P("expert", None, "stream"),
            P("expert", None, "stream"),
            P("expert", None, "stream"),
        ),
        out_specs=P(("stream", "expert"), None),
        check_vma=False,
    )
```

time: 173 us -> 146 us (0.84)
  the two profiles are of different devices: /device:TPU:1 before, /device:TPU:72 now
where the time goes in v2:
time: 146 us; the launch traced here: 145 us
  Pallas kernels  142 us (97%)
  local copies, waits for them, and re-layouts  3.03 us (2%)
    pallas_call x1, Pallas kernels, local(): pl.pallas_call(kernel, out_shape=jax.ShapeDtypeStruct((64, 2048), BF16),...  142 us
    unnamed x7, local copies, waits for them, and re-layouts  3.03 us

profile of v2, /device:TPU:72, one launch (start us, length us, event | category | flops | bytes accessed | tf_op | source)
XLA Modules:
  0.0 145.5 jit_solution(1535603680032021772)
XLA Ops:
  0.0 0.0 copy-start.1
  0.0 0.0 copy-start
  0.0 0.7 copy-done.1
  0.7 0.0 copy-done
  0.7 0.0 copy-start.2
  0.7 0.7 copy-done.2
  1.4 0.7 pad_maximum_fusion.meta
  2.1 141.7 %experts.1 = bf16[64,2048]{1,0:T(8,128)(2,1)} custom-call(bf16[64,2048]{1,0:T(8,128)(2,1)} %tok.1, f32[16,128]{1,0:T(8,128)} %pad_maximum_fusion.meta, f32[16]{0:T(128)} %bitcast.11, f32[16]{0:T(128)} %bitcast.12, f32[16]{0:T(128)} %bitcast.13, bf16[2048,128]{1,0:T(8,128)(2,1)} %bitcast.8, bf16[2048,128]{1,0:T(8,128)(2,1)} %bitcast.9, bf16[2048,128]{1,0:T(8,128)(2,1)} %bitcast.10), custom_call_target="tpu_custom_call" | custom-call | tf_op jit(solution)/shard_map/experts/pallas_call | solution.py:425
  143.8 1.7 %copy.12 = bf16[64,2048]{1,0:T(8,128)(2,1)} copy(bf16[64,2048]{1,0:T(8,128)(2,1)} %experts.1) | data formatting | bytes 524288
  (2 shorter events, 0.0 us)
Async XLA Ops:
  0.0 0.7 copy-start.1
  0.0 0.7 copy-start
  0.7 0.7 copy-start.2

commit v3 on v2

--- a/solution.py
+++ b/solution.py
@@ -14,6 +14,9 @@
 DN_CHUNKS = 2
 CHUNKS = GU_CHUNKS + DN_CHUNKS
 TOKEN_TIMES = (8.0, 17.0, 25.0, 32.0)
+PAIRS = (3, 2, 1, 0)
+LATE = 1
+BACK_WINDOW = 2
 A_FIRST, A_STEP, A_FAR = 6.0, 4.0, 5.0
 SWAP_WINDOW = 2
 OWN_WINDOW = 2
@@ -25,7 +28,7 @@
 
 
 def kernel(
-    tok, meta, sg, su, sd, gq, uq, dq, o_ref,
+    tok, gates, ids, slots, sg, su, sd, gq, uq, dq, o_ref,
     tk, mt, mz, ob, ib, gu, dn, lg, ld, hid, lhs, ans, ret, wh, wl, pt, rs_out, rs_in,
     w_send, w_recv, t_send, t_recv, m_send, m_recv, n_send, n_recv, a_send, a_recv, b_send, b_recv, r_send, r_recv,
 ):
@@ -72,8 +75,13 @@
         pl.when(jnp.logical_not(swaps))(lambda: fill(gu.at[0], dn.at[0]))
 
     tk[0] = tok[...]
-    mt[0] = meta[...]
-    mz[0] = meta[...]
+    chosen, place = ids[...], slots[...]
+    code = ((chosen % 2) * 4 + (chosen // 2) % 4) * 64 + (chosen // 8) * 8 + place
+    code = jnp.where(place >= 0, code, -1).astype(F32)
+    info = jnp.concatenate([code, gates[...]], axis=0)
+    info = jnp.concatenate([info, info], axis=1)
+    mt[0] = info
+    mz[0] = info
     for i in range(CHUNKS):
         dequantize(i)
     pl.semaphore_wait(barrier, len(peers))
@@ -257,59 +265,74 @@
         swapped += [(t, own_round, i), (t + B_NEXT, forward_round, i), (t + B_NEXT + B_FAR, far_round, i)]
     order = lambda event: event[0]
     kept, swapped = sorted(kept, key=order), sorted(swapped, key=order)
-    since = -1.0
-    for s, until in enumerate(TOKEN_TIMES + (1e9,)):
-        pl.when(jnp.logical_not(swaps))(run([e[1:] for e in kept if since <= e[0] < until]))
-        pl.when(swaps)(run([e[1:] for e in swapped if since <= e[0] < until]))
-        since = until
+    def part(events, since, until):
+        return run([e[1:] for e in events if since <= e[0] < until])
+
+    late = [(forward_round, CHUNKS - 1), (far_round, CHUNKS - 1)][2 - LATE :]
+    swapped = [e for e in swapped if e[1:] not in late]
+    times = (-1.0,) + TOKEN_TIMES + (1e9,)
+    for s in range(5):
+        pl.when(jnp.logical_not(swaps))(part(kept, times[s], times[s + 1]))
+        pl.when(swaps)(part(swapped, times[s], times[s + 1]))
+        if s == 3:
+            for k in range(1, 8):
+                meta_z(k).wait_recv()
+            for p in range(4):
+                weigh(1, p)
         if s < 4:
             token_round(s)
-    for i in range(GU_CHUNKS):
-        for r in range(4):
-            share(i, r).wait_recv()
-    for p in range(4):
-        for k in range(1, 8):
-            there(p, k).wait_recv()
-
-    for k in range(1, 8):
-        meta_z(k).wait_recv()
-    for p in range(4):
-        weigh(1, p)
-
-    def hidden_step(s, carry):
-        for m in range(2):
+
+    def hidden(m, since, until):
+        def hidden_step(s, carry):
             rows = pl.ds(m * 256, 256)
             both = jnp.dot(ib[rows, :], gu[s], preferred_element_type=F32)
             g, u = both[:, :128], both[:, 128:]
             hid[rows, pl.ds(pl.multiple_of(s * 128, 128), 128)] = g / (1.0 + jnp.exp(-g)) * u
-        return carry
-
-    lax.fori_loop(0, 8, hidden_step, 0)
-    for i in range(GU_CHUNKS, CHUNKS):
+            return carry
+
+        for p in (2 * m, 2 * m + 1):
+            if since == 0:
+                for k in range(1, 8):
+                    there(p, k).wait_recv()
+        lax.fori_loop(since, until, hidden_step, 0)
+
+    for i in range(GU_CHUNKS):
         for r in range(4):
             share(i, r).wait_recv()
-
-    for p in (3, 2, 1, 0):
-        for h in range(2):
+    hidden(0, 0, 4)
+    pl.when(swaps)(run(late[:-1]))
+    hidden(0, 4, 8)
+    pl.when(swaps)(run(late[-1:]))
+    hidden(1, 0, 8)
+
+    for h in range(2):
+        for i in range(GU_CHUNKS + h * (DN_CHUNKS // 2), GU_CHUNKS + (h + 1) * (DN_CHUNKS // 2)):
+            for r in range(4):
+                share(i, r).wait_recv()
+        for p in range(4):
             if h == 0:
-                lhs[...] = hid[pl.ds(p * 128, 128), :].astype(BF16)
+                lhs[pl.ds(p * 128, 128), :] = hid[pl.ds(p * 128, 128), :].astype(BF16)
             else:
                 for q in range(4):
                     first = q * 128 + p * 32
-                    part = [hid[pl.ds(first + g, 8), :] for g in (0, 16, 8, 24)]
-                    lhs[pl.ds(q * 32, 32), :] = jnp.concatenate(part, axis=0).astype(BF16)
-
-            def answer_step(c, carry, h=h, p=p):
-                first = pl.multiple_of(c * 256, 256)
-                down = jnp.concatenate([dn[s, pl.ds(h * 1024 + first, 256), :] for s in range(8)], axis=1)
-                a = lax.dot_general(lhs[...], down, (((1,), (1,)), ((), ())), preferred_element_type=F32)
-                ans[h, pl.ds(p * 128, 128), pl.ds(first, 256)] = a.astype(BF16)
-                return carry
-
-            lax.fori_loop(0, 4, answer_step, 0)
+                    some = [hid[pl.ds(first + g, 8), :] for g in (0, 16, 8, 24)]
+                    lhs[pl.ds(p * 128 + q * 32, 32), :] = jnp.concatenate(some, axis=0).astype(BF16)
+
+        def answer_step(c, carry, h=h):
+            first = pl.multiple_of(c * 256, 256)
+            down = jnp.concatenate([dn[s, pl.ds(h * 1024 + first, 256), :] for s in range(8)], axis=1)
+            for m in range(2):
+                rows = pl.ds(m * 256, 256)
+                a = lax.dot_general(lhs[rows, :], down, (((1,), (1,)), ((), ())), preferred_element_type=F32)
+                ans[h, rows, pl.ds(first, 256)] = a.astype(BF16)
+            return carry
+
+        lax.fori_loop(0, 4, answer_step, 0)
+        for p in range(4):
+            ret[h, pl.ds(p * 128, 16), :] = ans[h, pl.ds(p * 128, 16), :]
+        for p in PAIRS[:BACK_WINDOW]:
             for k in Z_ORDER:
                 back(h, p, k).start()
-            ret[h, pl.ds(p * 128, 16), :] = ans[h, pl.ds(p * 128, 16), :]
 
     def sum_up(h, s):
         rows = pl.ds(0, 32 if s == 0 else 64)
@@ -324,6 +347,9 @@
     def combine(h, p):
         for k in range(1, 8):
             back(h, p, k).wait_recv()
+        for later in PAIRS[PAIRS.index(p) + BACK_WINDOW :][:1]:
+            for k in Z_ORDER:
+                back(h, later, k).start()
         for c in range(2):
             cols = pl.ds(c * 512, 512)
             r = ret[h, pl.ds(p * 128, 128), cols]
@@ -415,17 +441,13 @@
     up_scale,
     down_scale,
 ):
-    y_of = (expert_ids % 2) * 4 + (expert_ids // 2) % 4
-    code = jnp.where(slot_index >= 0, y_of * 64 + (expert_ids // 8) * 8 + slot_index, -1).astype(F32)
-    info = jnp.concatenate([code, route_gates], axis=1).T
-    info = jnp.concatenate([info, info], axis=1)
     vmem = pl.BlockSpec(memory_space=pltpu.VMEM)
     smem = pl.BlockSpec(memory_space=pltpu.SMEM)
     dma = pltpu.SemaphoreType.DMA
     return pl.pallas_call(
         kernel,
         out_shape=jax.ShapeDtypeStruct((64, 2048), BF16),
-        in_specs=[vmem, vmem, smem, smem, smem, vmem, vmem, vmem],
+        in_specs=[vmem] * 4 + [smem] * 3 + [vmem] * 3,
         out_specs=vmem,
         scratch_shapes=[
             pltpu.VMEM((8, 64, 2048), BF16),
@@ -438,7 +460,7 @@
             pltpu.VMEM((2048, 256), BF16),
             pltpu.VMEM((2048, 128), BF16),
             pltpu.VMEM((512, 1024), F32),
-            pltpu.VMEM((128, 1024), BF16),
+            pltpu.VMEM((512, 1024), BF16),
             pltpu.VMEM((2, 512, 1024), BF16),
             pltpu.VMEM((2, 512, 1024), BF16),
             pltpu.VMEM((2, 4, 128, 128), BF16),
@@ -467,7 +489,9 @@
         name="experts",
     )(
         tokens,
-        info,
+        route_gates.T,
+        expert_ids.T,
+        slot_index.T,
         gate_scale.reshape(16),
         up_scale.reshape(16),
         down_scale.reshape(16),

time: 146 us -> 136 us (0.932)
  the two profiles are of different devices: /device:TPU:72 before, /device:TPU:1 now
where the time goes in v3:
time: 136 us; the launch traced here: 135 us
  Pallas kernels  134 us (99%)
  local copies, waits for them, and re-layouts  1.67 us (1%)
    pallas_call x1, Pallas kernels, local(): pl.pallas_call(kernel, out_shape=jax.ShapeDtypeStruct((64, 2048), BF16),...  134 us

profile of v3, /device:TPU:1, one launch (start us, length us, event | category | flops | bytes accessed | tf_op | source)
XLA Modules:
  0.0 135.4 jit_solution(14427920702151291406)
XLA Ops:
  0.0 133.7 %experts.1 = bf16[64,2048]{1,0:T(8,128)(2,1)} custom-call(bf16[64,2048]{1,0:T(8,128)(2,1)} %tok.1, f32[8,64]{1,0:T(8,128)} %bitcast.12, s32[8,64]{1,0:T(8,128)} %bitcast.13, s32[8,64]{1,0:T(8,128)} %bitcast.14, f32[16]{0:T(128)} %bitcast.15, f32[16]{0:T(128)} %bitcast.16, f32[16]{0:T(128)} %bitcast.17, bf16[2048,128]{1,0:T(8,128)(2,1)} %bitcast.9, ...), custom_call_target="tpu_custom_call" | custom-call | tf_op jit(solution)/shard_map/experts/pallas_call | solution.py:447
  133.7 1.7 %copy.12 = bf16[64,2048]{1,0:T(8,128)(2,1)} copy(bf16[64,2048]{1,0:T(8,128)(2,1)} %experts.1) | data formatting | bytes 524288

commit v4 on v3

--- a/solution.py
+++ b/solution.py
@@ -305,34 +305,33 @@
     pl.when(swaps)(run(late[-1:]))
     hidden(1, 0, 8)
 
-    for h in range(2):
-        for i in range(GU_CHUNKS + h * (DN_CHUNKS // 2), GU_CHUNKS + (h + 1) * (DN_CHUNKS // 2)):
-            for r in range(4):
-                share(i, r).wait_recv()
-        for p in range(4):
+    for m, h in ((1, 0), (1, 1), (0, 0), (0, 1)):
+        if m == 1:
+            for i in range(GU_CHUNKS + h * (DN_CHUNKS // 2), GU_CHUNKS + (h + 1) * (DN_CHUNKS // 2)):
+                for r in range(4):
+                    share(i, r).wait_recv()
+        for p in (2 * m, 2 * m + 1):
             if h == 0:
-                lhs[pl.ds(p * 128, 128), :] = hid[pl.ds(p * 128, 128), :].astype(BF16)
+                lhs[pl.ds((p % 2) * 128, 128), :] = hid[pl.ds(p * 128, 128), :].astype(BF16)
             else:
                 for q in range(4):
                     first = q * 128 + p * 32
                     some = [hid[pl.ds(first + g, 8), :] for g in (0, 16, 8, 24)]
-                    lhs[pl.ds(p * 128 + q * 32, 32), :] = jnp.concatenate(some, axis=0).astype(BF16)
-
-        def answer_step(c, carry, h=h):
+                    lhs[pl.ds((p % 2) * 128 + q * 32, 32), :] = jnp.concatenate(some, axis=0).astype(BF16)
+
+        def answer_step(c, carry, h=h, m=m):
             first = pl.multiple_of(c * 256, 256)
             down = jnp.concatenate([dn[s, pl.ds(h * 1024 + first, 256), :] for s in range(8)], axis=1)
-            for m in range(2):
-                rows = pl.ds(m * 256, 256)
-                a = lax.dot_general(lhs[rows, :], down, (((1,), (1,)), ((), ())), preferred_element_type=F32)
-                ans[h, rows, pl.ds(first, 256)] = a.astype(BF16)
+            a = lax.dot_general(lhs[...], down, (((1,), (1,)), ((), ())), preferred_element_type=F32)
+            ans[h, pl.ds(m * 256, 256), pl.ds(first, 256)] = a.astype(BF16)
             return carry
 
         lax.fori_loop(0, 4, answer_step, 0)
-        for p in range(4):
+        for p in (2 * m + 1, 2 * m):
             ret[h, pl.ds(p * 128, 16), :] = ans[h, pl.ds(p * 128, 16), :]
-        for p in PAIRS[:BACK_WINDOW]:
-            for k in Z_ORDER:
-                back(h, p, k).start()
+            if PAIRS.index(p) < BACK_WINDOW:
+                for k in Z_ORDER:
+                    back(h, p, k).start()
 
     def sum_up(h, s):
         rows = pl.ds(0, 32 if s == 0 else 64)
@@ -354,78 +353,76 @@
             cols = pl.ds(c * 512, 512)
             r = ret[h, pl.ds(p * 128, 128), cols]
             high = jnp.dot(wh[h, p], r, preferred_element_type=F32)
-            pt[h, :, cols] = high + jnp.dot(wl[h, p], r, preferred_element_type=F32)
-
-    def add_up(h, s, first):
+            pt[h, p, :, cols] = high + jnp.dot(wl[h, p], r, preferred_element_type=F32)
+
+    def add_up(h, s, p):
         sum_up(h, s - 1).wait_recv()
         if s == 1:
-            rs_out[h, 0, s, 0:32, :] = (pt[h, first : first + 32, :] + rs_in[h, 0, 0, 0:32, :].astype(F32)).astype(BF16)
-            rs_out[h, 0, s, 32:64, :] = pt[h, first + 32 : first + 64, :].astype(BF16)
+            rs_out[h, 0, s, 0:32, :] = (pt[h, p, 0:32, :] + rs_in[h, 0, 0, 0:32, :].astype(F32)).astype(BF16)
+            rs_out[h, 0, s, 32:64, :] = pt[h, p, 32:64, :].astype(BF16)
         else:
-            rs_out[h, 0, s] = (pt[h, first : first + 64, :] + rs_in[h, 0, s - 1].astype(F32)).astype(BF16)
+            rs_out[h, 0, s] = (pt[h, p, 0:64, :] + rs_in[h, 0, s - 1].astype(F32)).astype(BF16)
         sum_up(h, s).start()
 
-    def add_down(h, s, first):
+    def add_down(h, s, p):
         sum_down(h, s - 1).wait_recv()
         if s == 1:
-            rs_out[h, 1, s, 0:32, :] = pt[h, first : first + 32, :].astype(BF16)
-            last = pt[h, first + 32 : first + 64, :] + rs_in[h, 1, 0, 32:64, :].astype(F32)
+            rs_out[h, 1, s, 0:32, :] = pt[h, p, 64:96, :].astype(BF16)
+            last = pt[h, p, 96:128, :] + rs_in[h, 1, 0, 32:64, :].astype(F32)
             rs_out[h, 1, s, 32:64, :] = last.astype(BF16)
         else:
-            rs_out[h, 1, s] = (pt[h, first : first + 64, :] + rs_in[h, 1, s - 1].astype(F32)).astype(BF16)
+            rs_out[h, 1, s] = (pt[h, p, 64:128, :] + rs_in[h, 1, s - 1].astype(F32)).astype(BF16)
         sum_down(h, s).start()
+
+    def gathers_sent():
+        @pl.when(swaps)
+        def _():
+            for i in range(CHUNKS):
+                swap(i).wait_send()
+
+        for i in range(CHUNKS):
+            own_up(i).wait_send()
+            own_down(i).wait_send()
+            on_up(i).wait_send()
+            on_down(i).wait_send()
+            for r in range(4):
+                share(i, r).wait_send()
+        for s in range(4):
+            tok_up(s).wait_send()
+            tok_down(s).wait_send()
+            meta_up(s).wait_send()
+            if s < 3:
+                meta_down(s).wait_send()
+        for k in range(1, 8):
+            meta_z(k).wait_send()
+            for p in range(4):
+                there(p, k).wait_send()
 
     for h in range(2):
         combine(h, 3)
-        rs_out[h, 0, 0, 0:32, :] = pt[h, 64:96, :].astype(BF16)
-        rs_out[h, 1, 0, 32:64, :] = pt[h, 96:128, :].astype(BF16)
+        rs_out[h, 0, 0, 0:32, :] = pt[h, 3, 64:96, :].astype(BF16)
+        rs_out[h, 1, 0, 32:64, :] = pt[h, 3, 96:128, :].astype(BF16)
         sum_up(h, 0).start()
         sum_down(h, 0).start()
-    for h in range(2):
-        add_up(h, 1, 0)
-    for h in range(2):
-        combine(h, 2)
-        add_down(h, 1, 64)
-        add_up(h, 2, 0)
-    for h in range(2):
-        combine(h, 1)
-        add_down(h, 2, 64)
-        add_up(h, 3, 0)
-    for h in range(2):
-        combine(h, 0)
-        add_down(h, 3, 64)
+    for s, p in ((1, 2), (2, 1), (3, 0)):
+        for h in range(2):
+            combine(h, p)
+            add_down(h, s, p)
+            add_up(h, s, p + 1)
+        if s == 2:
+            gathers_sent()
     for h in range(2):
         sum_up(h, 3).wait_recv()
         sum_down(h, 3).wait_recv()
-        total = pt[h, 0:64, :] + rs_in[h, 0, 3].astype(F32) + rs_in[h, 1, 3].astype(F32)
+        total = pt[h, 0, 0:64, :] + rs_in[h, 0, 3].astype(F32) + rs_in[h, 1, 3].astype(F32)
         o_ref[:, h * 1024 : h * 1024 + 1024] = total.astype(BF16)
 
-    @pl.when(swaps)
-    def _():
-        for i in range(CHUNKS):
-            swap(i).wait_send()
-
-    for i in range(CHUNKS):
-        own_up(i).wait_send()
-        own_down(i).wait_send()
-        on_up(i).wait_send()
-        on_down(i).wait_send()
-        for r in range(4):
-            share(i, r).wait_send()
-    for s in range(4):
-        tok_up(s).wait_send()
-        tok_down(s).wait_send()
-        meta_up(s).wait_send()
-        if s < 3:
-            meta_down(s).wait_send()
-        for h in range(2):
+    for h in range(2):
+        for s in range(4):
             sum_up(h, s).wait_send()
             sum_down(h, s).wait_send()
-    for k in range(1, 8):
-        meta_z(k).wait_send()
         for p in range(4):
-            there(p, k).wait_send()
-            for h in range(2):
+            for k in range(1, 8):
                 back(h, p, k).wait_send()
 
 
@@ -460,12 +457,12 @@
             pltpu.VMEM((2048, 256), BF16),
             pltpu.VMEM((2048, 128), BF16),
             pltpu.VMEM((512, 1024), F32),
-            pltpu.VMEM((512, 1024), BF16),
+            pltpu.VMEM((256, 1024), BF16),
             pltpu.VMEM((2, 512, 1024), BF16),
             pltpu.VMEM((2, 512, 1024), BF16),
             pltpu.VMEM((2, 4, 128, 128), BF16),
             pltpu.VMEM((2, 4, 128, 128), BF16),
-            pltpu.VMEM((2, 128, 1024), F32),
+            pltpu.VMEM((2, 4, 128, 1024), F32),
             pltpu.VMEM((2, 2, 4, 64, 1024), BF16),
             pltpu.VMEM((2, 2, 4, 64, 1024), BF16),
             dma((CHUNKS, 9)),

time: 136 us -> 135 us (level)
  no operation moved by 1% of the time
where the time goes in v4:
time: 135 us
  Pallas kernels  133 us (99%)
  local copies, waits for them, and re-layouts  1.67 us (1%)
    pallas_call x1, Pallas kernels, local(): pl.pallas_call(kernel, out_shape=jax.ShapeDtypeStruct((64, 2048), BF16),...  133 us

profile of v4, /device:TPU:1, one launch (start us, length us, event | category | flops | bytes accessed | tf_op | source)
XLA Modules:
  0.0 134.7 jit_solution(14239551737622798260)
XLA Ops:
  0.0 133.0 %experts.1 = bf16[64,2048]{1,0:T(8,128)(2,1)} custom-call(bf16[64,2048]{1,0:T(8,128)(2,1)} %tok.1, f32[8,64]{1,0:T(8,128)} %bitcast.12, s32[8,64]{1,0:T(8,128)} %bitcast.13, s32[8,64]{1,0:T(8,128)} %bitcast.14, f32[16]{0:T(128)} %bitcast.15, f32[16]{0:T(128)} %bitcast.16, f32[16]{0:T(128)} %bitcast.17, bf16[2048,128]{1,0:T(8,128)(2,1)} %bitcast.9, ...), custom_call_target="tpu_custom_call" | custom-call | tf_op jit(solution)/shard_map/experts/pallas_call | solution.py:444
  133.0 1.7 %copy.12 = bf16[64,2048]{1,0:T(8,128)(2,1)} copy(bf16[64,2048]{1,0:T(8,128)(2,1)} %experts.1) | data formatting | bytes 524288
